TPU v7x, 32 devices: a whole 2x2x4 slice. The times are simulated.
32 devices in a mesh: front: 2 (over x), row: 4 (over y, core), col: 4 (over z).
Axes of the slice: x: 2, y: 2, z: 4, core: 2. Of those that a mesh axis runs over, the one named last changes fastest.
Arguments:
- child_fronts: float32 [32, 1536, 1536], P(('front', 'row', 'col')), may hold values from -6 to 103.97959, as said below
- parent_entries: float32 [2, 4096, 4096], P('front', 'row', 'col'), may hold values from -6 to 166, as said below
- tile_map: int32 [32, 8], P(('front', 'row', 'col')), may hold values from 0 to 31, as said below
- parent_group: int32 [32], P(('front', 'row', 'col')), may hold values from 0 to 1, as said below
Outputs:
- child_factor: float32 [32, 1536, 512], P(('front', 'row', 'col'))
- parent_factor: float32 [2, 4096, 4096], P('front', 'row', 'col')
Inputs may be any that keep to these rules, and one draw needn't show every extreme that they name: `child_fronts`: each child front is symmetric positive definite. `parent_entries`: each parent's entries are symmetric, and every assembled parent front is positive definite. `tile_map`: each row is increasing and names exactly 2 tiles among each 8 consecutive tile numbers that start at a multiple of 8. `parent_group`: children are numbered in the order of the devices; in each run of 16 consecutive children, exactly 8 have each parent.
All inputs are finite; a program needn't handle non-finite values.
Results may differ from a plain program's by a relative error of at most 0.0001.
Values sent between devices are 32-bit elements; how exact they have to be, the bound alone decides.
A program may use at most 192 MiB of HBM per device.

v0:
```python
import jax
import jax.numpy as jnp
from jax import lax
from jax.sharding import PartitionSpec as P

TILE = 128


def broadcast(array, axis, root):
    mine = lax.axis_index(axis) == root
    return lax.psum(jnp.where(mine, array, jnp.zeros_like(array)), axis)


def right_solve(pivot_factor, matrix):
    return lax.linalg.triangular_solve(
        pivot_factor, matrix, left_side=False, lower=True, transpose_a=True
    )


def local(child_fronts, parent_entries, tile_map, parent_group):
    child_front = child_fronts[0]
    pivot_count = child_front.shape[0] - tile_map.shape[1] * TILE
    border_tiles = tile_map.shape[1]
    pivot_factor = jnp.linalg.cholesky(child_front[:pivot_count, :pivot_count])
    child_panel = right_solve(pivot_factor, child_front[pivot_count:, :pivot_count])
    update = child_front[pivot_count:, pivot_count:] - jnp.dot(
        child_panel, child_panel.T, precision=lax.Precision.HIGHEST
    )
    factor_out = jnp.concatenate([pivot_factor, child_panel], 0)[None]
    row_count = lax.axis_size("row")
    col_count = lax.axis_size("col")
    front_count = lax.axis_size("front")
    row_here = lax.axis_index("row")
    col_here = lax.axis_index("col")
    border = update.shape[0]
    piece_rows = border // row_count
    pieces = update.reshape(row_count, piece_rows, col_count, piece_rows).transpose(0, 2, 1, 3)
    pieces = pieces.reshape(row_count * col_count, piece_rows, piece_rows)
    label_row = jnp.concatenate([tile_map[0].astype(jnp.float32), parent_group.astype(jnp.float32)])
    labels = jnp.broadcast_to(label_row[None, :], (row_count * col_count, border_tiles + 1))
    arrived, arrived_labels = (
        lax.all_to_all(pieces, ("row", "col"), split_axis=0, concat_axis=0, tiled=True),
        lax.all_to_all(labels, ("row", "col"), split_axis=0, concat_axis=0, tiled=True),
    )
    groups = arrived_labels[:, border_tiles].astype(jnp.int32)
    arrange = jnp.argsort(groups, stable=True)
    per_parent = arrived.shape[0] // front_count
    regrouped = arrived[arrange].reshape(front_count, per_parent, piece_rows, piece_rows)
    regrouped_labels = arrived_labels[arrange].reshape(front_count, per_parent, border_tiles + 1)
    landed, landed_labels = (
        lax.all_to_all(regrouped, "front", split_axis=0, concat_axis=0, tiled=True),
        lax.all_to_all(regrouped_labels, "front", split_axis=0, concat_axis=0, tiled=True),
    )
    landed = landed.reshape(-1, piece_rows, piece_rows)
    tile_ids = landed_labels.reshape(-1, border_tiles + 1)[:, :border_tiles].astype(jnp.int32)
    local_block = parent_entries[0]
    local_tiles = local_block.shape[0] // TILE
    per_block = border_tiles // row_count
    row_tiles = (
        lax.dynamic_slice_in_dim(tile_ids, row_here * per_block, per_block, 1)
        - row_here * local_tiles
    )
    col_tiles = (
        lax.dynamic_slice_in_dim(tile_ids, col_here * per_block, per_block, 1)
        - col_here * local_tiles
    )
    row_starts = row_tiles * TILE
    col_starts = col_tiles * TILE
    piece_count = landed.shape[0]

    def add_piece(index, block):
        piece = landed[index]
        for first in range(per_block):
            for second in range(per_block):
                start_row = row_starts[index, first]
                start_col = col_starts[index, second]
                tile = piece[first * TILE : (first + 1) * TILE, second * TILE : (second + 1) * TILE]
                current = lax.dynamic_slice(block, (start_row, start_col), (TILE, TILE))
                block = lax.dynamic_update_slice(block, current + tile, (start_row, start_col))
        return block

    local_block = lax.fori_loop(0, piece_count, add_piece, local_block)
    diag_block = broadcast(local_block, ("row", "col"), 0)
    corner = jnp.linalg.cholesky(diag_block)
    row_source = broadcast(local_block, "col", 0)
    col_source = broadcast(local_block, "row", 0)
    row_share = local_block.shape[0] // col_count
    col_share = local_block.shape[1] // row_count
    part_row = right_solve(
        corner, lax.dynamic_slice_in_dim(row_source, col_here * row_share, row_share, 0)
    )
    w_row = lax.all_gather(part_row, "col", axis=0, tiled=True)
    part_col = right_solve(
        corner, lax.dynamic_slice_in_dim(col_source, row_here * col_share, col_share, 1).T
    )
    w_col = lax.all_gather(part_col, "row", axis=0, tiled=True)
    trailing = local_block - lax.dot_general(
        w_row, w_col, (((1,), (1,)), ((), ())), precision=lax.Precision.HIGHEST
    )
    result = jnp.where(col_here == 0, w_row, jnp.where(row_here == 0, w_col.T, trailing))
    result = jnp.where((row_here == 0) & (col_here == 0), corner, result)
    return (factor_out, result[None])


def solution(mesh):
    in_specs = (
        P(("front", "row", "col"), None, None),
        P("front", "row", "col"),
        P(("front", "row", "col"), None),
        P(("front", "row", "col")),
    )
    out_specs = (P(("front", "row", "col"), None, None), P("front", "row", "col"))
    return jax.shard_map(local, mesh=mesh, in_specs=in_specs, out_specs=out_specs, check_vma=False)
```

profile of v0, /device:TPU:17, one launch (start us, length us, event | category | flops | bytes accessed | tf_op | source)
XLA Modules:
  0.0 1394.5 jit_solution(7949320384899144387)
XLA Ops:
  7.2 4.8 copy.314
  13.3 6.5 all-to-all-start
  19.8 9.6 copy.124
  32.6 11.7 cholesky.279
  44.3 9.8 custom-call.80
  54.9 11.7 cholesky.293
  66.7 10.0 custom-call.81
  77.4 11.7 cholesky.314
  89.9 9.8 custom-call.82
  100.3 11.7 cholesky.329
  116.1 12.7 fusion.31
  128.8 8.3 while.19
  137.2 39.3 %custom-call.71 = f32[4,128,128]{1,2,0:T(8,128)S(1)} custom-call(f32[4,128,128]{2,1,0:T(8,128)S(1)} %get-tuple-element.118), custom_call_target="InvertDiagBlocksLowerTriangular" | custom-call | tf_op jit(solution)/shard_map/triangular_solve | solution.py:15
  185.6 10.1 slice_subtract_fusion
  195.8 5.6 reshape.129
  201.4 5.2 copy.133
  206.6 6.0 all-to-all-start.2
  215.2 87.7 %all-to-all-done.2 = f32[16,256,256]{2,1,0:T(8,128)} async-done(((f32[16,256,256]{2,1,0:T(8,128)}), f32[16,256,256]{2,1,0:T(8,128)}, u32[]{:S(2)}, u32[]{:S(2)}) %all-to-all-start.2) | async-done | bytes 4194336 | tf_op jit(solution)/shard_map/all_to_all | solution.py:42
  306.1 5.0 gather_fusion.1
  311.1 5.6 all-to-all-start.3
  317.1 46.2 %all-to-all-done.3 = f32[2,8,256,256]{3,2,1,0:T(8,128)} async-done(((f32[2,8,256,256]{3,2,1,0:T(8,128)}), f32[2,8,256,256]{3,2,1,0:T(8,128)}, u32[]{:S(2)}, u32[]{:S(2)}) %all-to-all-start.3) | async-done | bytes 4194336 | tf_op jit(solution)/shard_map/all_to_all | solution.py:51
  363.3 392.1 %while.18 = (s32[]{:T(128)}, f32[1024,1024]{1,0:T(8,128)}, s32[16,2]{0,1:T(2,128)S(1)}, s32[16,2]{0,1:T(2,128)S(1)}, f32[16,256,256]{2,1,0:T(8,128)}, /*index=5*/s32[]{:T(128)}, s32[]{:T(128)}, s32[]{:T(128)}) while((s32[]{:T(128)}, f32[1024,1024]{1,0:T(8,128)}, s32[16,2]{0,1:T(2,128)S(1)}, s32[16,2]{0,1:T(2,128)S(1)}, ...), condition=%wide.region_10.14_spmd, body=%wide.region_9.13_spmd.sunk | while | flops 65550 | bytes 1835317 | solution.py:82
  755.4 5.4 copy.136
  760.7 7.8 broadcast_select_fusion
  770.1 114.7 %all-reduce.6.cloned.1.call-done = f32[1024,1024]{0,1:T(8,128)} async-done(((f32[1024,1024]{0,1:T(8,128)}), f32[1024,1024]{0,1:T(8,128)}) %all-reduce.6.cloned.1.call-update) | async-done | bytes 4194320 | tf_op jit(solution)/shard_map/psum | solution.py:11
  884.8 5.7 copy.137
  890.5 4.4 fusion.3
  896.9 11.7 cholesky.588
  908.6 9.8 custom-call.72
  922.4 11.7 cholesky.606
  937.2 9.8 custom-call.73
  952.5 11.7 cholesky.627
  965.0 9.8 custom-call.74
  979.4 11.7 cholesky.646
  991.9 9.8 custom-call.75
  1006.0 12.1 cholesky.665
  1018.9 9.8 custom-call.83
  1032.9 11.7 cholesky.681
  1045.4 9.8 custom-call.84
  1059.0 11.7 cholesky.697
  1071.5 9.8 custom-call.85
  1084.3 11.7 cholesky.711
  1106.7 4.8 fusion.4
  1111.5 29.0 %while.20 = (s32[]{:T(128)}, f32[1024,1024]{0,1:T(8,128)}, s32[8,2]{0,1:T(2,128)S(1)}, f32[8,128,128]{2,1,0:T(8,128)}, s32[]{:T(128)}) while((s32[]{:T(128)}, f32[1024,1024]{0,1:T(8,128)}, s32[8,2]{0,1:T(2,128)S(1)}, f32[8,128,128]{2,1,0:T(8,128)}, s32[]{:T(128)}) %tuple.153), condition=%wide.while_cond, body=%wide.while_body.sunk | while | flops 2 | bytes 393829 | solution.py:15
  1140.6 80.2 %custom-call.86 = f32[8,128,128]{1,2,0:T(8,128)} custom-call(f32[8,128,128]{2,1,0:T(8,128)} %get-tuple-element.125), custom_call_target="InvertDiagBlocksLowerTriangular" | custom-call | tf_op jit(solution)/shard_map/triangular_solve/custom-call.20 | solution.py:15
  1278.8 80.4 %all-gather.3.cloned.1.call-done = f32[1024,1024]{0,1:T(8,128)} async-done(((f32[256,1024]{0,1:T(8,128)}), f32[1024,1024]{0,1:T(8,128)}) %all-gather.3.cloned.1.call-update) | async-done | bytes 4194320 | tf_op jit(solution)/shard_map/all_gather | solution.py:92
  1359.2 23.0 %fusion.2 = f32[1,1024,1024]{1,2,0:T(8,128)} fusion(f32[1024,1024]{0,1:T(8,128)} %all-gather.3.cloned.1.call-done, f32[1024,1024]{1,0:T(8,128)} %all-gather.5.cloned.1.call-done, f32[1024,1024]{0,1:T(8,128)} %copy.136, f32[1024,1024]{0,1:T(8,128)} %constant_dynamic-update-slice_fusion.61, pred[]{:T(512)S(6)} %cholesky.725, pred[]{:T(512)S(6)} %eq.6, ...), kind=kOutput, calls=%fused_computation.19 | convolution fusion | flops 12892241920 | bytes 20971524 | tf_op jit(solution)/shard_map/dot_general | solution.py:97
  1382.1 5.3 copy.193
  (377 shorter events, 436.0 us)
Async XLA Ops:
  7.2 5.5 copy-start.5
  13.3 193.3 %all-to-all-start = ((f32[16,1,9]{2,1,0:T(1,128)}), f32[16,1,9]{2,1,0:T(1,128)S(1)}, u32[]{:S(2)}, u32[]{:S(2)}) async-start(f32[16,1,9]{2,1,0:T(1,128)} %broadcast_in_dim.21), calls=%async_computation | async-start | bytes 16384 | tf_op jit(solution)/shard_map/all_to_all | solution.py:43
  206.6 96.3 %all-to-all-start.2 = ((f32[16,256,256]{2,1,0:T(8,128)}), f32[16,256,256]{2,1,0:T(8,128)}, u32[]{:S(2)}, u32[]{:S(2)}) async-start(f32[16,256,256]{2,1,0:T(8,128)} %bitcast.281), calls=%async_computation.2 | async-start | bytes 8388608 | tf_op jit(solution)/shard_map/all_to_all | solution.py:42
  302.9 8.2 all-to-all-start.1
  311.1 52.2 %all-to-all-start.3 = ((f32[2,8,256,256]{3,2,1,0:T(8,128)}), f32[2,8,256,256]{3,2,1,0:T(8,128)}, u32[]{:S(2)}, u32[]{:S(2)}) async-start(f32[2,8,256,256]{3,2,1,0:T(8,128)} %bitcast.280), calls=%async_computation.3 | async-start | bytes 8388608 | tf_op jit(solution)/shard_map/all_to_all | solution.py:51
  316.7 568.0 %all-reduce.6.cloned.1.call-start = ((), (), s32[]{:S(2)}) async-start(), calls=%async_computation.4 | async-start | bytes 8388608 | tf_op jit(solution)/shard_map/psum | solution.py:11
  768.5 452.3 %all-reduce.10.cloned.1.call-start = ((), (), s32[]{:S(2)}) async-start(), calls=%async_computation.7 | async-start | bytes 8388608 | tf_op jit(solution)/shard_map/psum | solution.py:11
  769.3 474.3 %all-reduce.8.cloned.1.call-start = ((), (), s32[]{:S(2)}) async-start(), calls=%async_computation.5 | async-start | bytes 8388608 | tf_op jit(solution)/shard_map/psum | solution.py:11
  770.0 508.8 %all-gather.5.cloned.1.call-start = ((), (), s32[]{:S(2)}) async-start(), calls=%async_computation.8 | async-start | bytes 5242880 | tf_op jit(solution)/shard_map/all_gather | solution.py:96
  894.9 1.9 copy-start
  921.5 0.8 copy-start.3
  934.4 14.1 %copy-start.4 = (f32[896,128]{1,0:T(8,128)S(1)}, f32[896,128]{1,0:T(8,128)}, u32[]{:S(2)}) copy-start(f32[896,128]{1,0:T(8,128)} %copy-done.3) | copy-start | bytes 1376260
  1223.3 8.3 copy-start.2
  1243.2 116.0 %all-gather.3.cloned.1.call-start = ((), (), s32[]{:S(2)}) async-start(), calls=%async_computation.6 | async-start | bytes 5242880 | tf_op jit(solution)/shard_map/all_gather | solution.py:92
  1255.1 14.6 %copy-start.1 = (f32[512,512]{1,0:T(8,128)S(1)}, f32[512,512]{1,0:T(8,128)}, u32[]{:S(2)}) copy-start(f32[512,512]{1,0:T(8,128)} %get-tuple-element.194) | copy-start | bytes 3145732
Sparse Core Ops, SparseCore 0:
  768.6 116.0 all-reduce.5
  887.8 85.7 all-reduce.9
  976.0 154.3 all-reduce.7
  1243.3 35.4 all-gather.4
  1280.3 78.8 all-gather.2
where the time goes:
time: 1420 us; the launch traced here: 1390 us
  other arithmetic  466 us (33%)
  waiting for transfers between devices  331 us (23%)
  local copies, waits for them, and re-layouts  315 us (22%)
  loops' own time  120 us (8%)
  matrix products  117 us (8%)
  between operations  23 us (2%)
  starting transfers between devices  21.8 us (2%)
    dynamic_update_slice x64, local copies, waits for them, and re-layouts, add_piece(): lax.dynamic_update_slice(block, current + tile, (start_row, start_col))  182 us
    another operation x31, other arithmetic, local(): corner = jnp.linalg.cholesky(diag_block)  168 us
    another operation x7, other arithmetic, right_solve(): lax.linalg.triangular_solve(pivot_factor, matrix, left_side=False, lower=...  137 us
    another operation x1, loops' own time, local(): local_block = lax.fori_loop(0, piece_count, add_piece, local_block)  120 us
    psum x3, waiting for transfers between devices, broadcast(): return lax.psum(jnp.where(mine, array, jnp.zeros_like(array)), axis)  115 us
    all_to_all x1, waiting for transfers between devices, local(): lax.all_to_all(pieces, ('row', 'col'), split_axis=0, concat_axis=0, tiled...  87.7 us
    all_gather x1, waiting for transfers between devices, local(): w_row = lax.all_gather(part_row, 'col', axis=0, tiled=True)  80.4 us
    another operation x14, other arithmetic, local(): pivot_factor = jnp.linalg.cholesky(child_front[:pivot_count, :pivot_count])  78.8 us
  transfers between devices with their start and end apart: 9, of which 5 were waited for; matrix products, arithmetic and copies ran while one was open for 41% of the time, Pallas kernels for 0%

commit v1 on v0

v1 whole, which is shorter than its diff:
```python
import functools

import jax
import jax.numpy as jnp
from jax import lax
from jax.experimental import pallas as pl
from jax.experimental.pallas import tpu as pltpu
from jax.sharding import PartitionSpec as P

TILE = 128
NB = 16
F32 = jnp.float32
BF16 = jnp.bfloat16
NT = (((1,), (1,)), ((), ()))
TN = (((0,), (0,)), ((), ()))
PARAMS = pltpu.CompilerParams(vmem_limit_bytes=56 * 1024 * 1024)
VMEM = pl.BlockSpec(memory_space=pltpu.VMEM)
SMEM = pl.BlockSpec(memory_space=pltpu.SMEM)


def split(x):
    hi = x.astype(BF16)
    return hi, (x - hi.astype(F32)).astype(BF16)


def mxu(a, b, dims):
    return lax.dot_general(a, b, dims, preferred_element_type=F32)


def weights(hi, lo):
    top = jnp.concatenate([hi, hi], 1)
    return jnp.concatenate([top, jnp.concatenate([lo, jnp.zeros_like(lo)], 1)], 0)


def product(hi, lo, weight):
    both = mxu(jnp.concatenate([hi, lo], 1), weight, NT)
    return both[:, :TILE] + both[:, TILE:]


def product3(ah, al, bh, bl):
    return mxu(ah, bh, NT) + mxu(ah, bl, NT) + mxu(al, bh, NT)


def chol_inverse(work):
    rows = lax.broadcasted_iota(jnp.int32, (NB, TILE), 0)
    for start in range(0, TILE, NB):
        left = work[start : start + NB, :TILE]
        right = work[start : start + NB, TILE:]
        cols = [
            jnp.broadcast_to(left[:, start + b : start + b + 1], (NB, TILE)) for b in range(NB)
        ]
        for a in range(NB):
            scale = lax.rsqrt(cols[a][a : a + 1, :])
            factor = jnp.where(rows > a, cols[a] * scale, 0.0)
            pivot_left = left[a : a + 1, :] * scale
            pivot_right = right[a : a + 1, :] * scale
            left = jnp.where(rows == a, pivot_left, left - factor * pivot_left)
            right = jnp.where(rows == a, pivot_right, right - factor * pivot_right)
            for b in range(a + 1, NB):
                cols[b] = cols[b] - factor * (cols[b][a : a + 1, :] * scale)
        work[start : start + NB, :TILE] = left
        work[start : start + NB, TILE:] = right
        if start + NB < TILE:
            hi, lo = split(jnp.concatenate([left, right], 1))
            mine = jnp.concatenate([hi[:, :TILE], hi[:, :TILE], lo[:, :TILE]], 0)
            change = mxu(mine, jnp.concatenate([hi, lo, hi], 0), TN)
            work[start + NB :, :] = work[start + NB :, :] - change[start + NB :, :]


def factor_loop(src, out, hi, lo, inv_hi, inv_lo, work, col, blocks, chunk):
    total = src.shape[0]
    row_id = lax.broadcasted_iota(jnp.int32, (TILE, TILE), 0)
    col_id = lax.broadcasted_iota(jnp.int32, (TILE, TILE), 1)

    def step(k, carry):
        here = pl.ds(pl.multiple_of(k * TILE, TILE), TILE)
        col[...] = src[:, here]

        def earlier(m, carry):
            there = pl.ds(pl.multiple_of(m * TILE, TILE), TILE)
            weight = weights(hi[here, there], lo[here, there])
            for first in range(0, total, chunk):
                part = pl.ds(first, chunk)
                col[part, :] = col[part, :] - product(hi[part, there], lo[part, there], weight)
            return carry

        lax.fori_loop(0, k, earlier, 0)
        work[:, :TILE] = col[here, :]
        work[:, TILE:] = jnp.where(row_id == col_id, 1.0, 0.0).astype(F32)
        chol_inverse(work)
        inverse_hi, inverse_lo = split(work[:, TILE:])
        if inv_hi is not None:
            inv_hi[k] = inverse_hi
            inv_lo[k] = inverse_lo
        weight = weights(inverse_hi, inverse_lo)
        for first in range(0, total, chunk):
            part = pl.ds(first, chunk)
            a_hi, a_lo = split(col[part, :])
            panel = product(a_hi, a_lo, weight)
            ids = lax.broadcasted_iota(jnp.int32, (chunk, TILE), 0) + first
            panel = jnp.where(ids >= k * TILE, panel, 0.0)
            out[part, here] = panel
            p_hi, p_lo = split(panel)
            hi[part, here] = p_hi
            lo[part, here] = p_lo
        lower = jnp.where(row_id >= col_id, work[:, :TILE].T, 0.0)
        out[here, here] = lower
        d_hi, d_lo = split(lower)
        hi[here, here] = d_hi
        lo[here, here] = d_lo
        return carry

    lax.fori_loop(0, blocks, step, 0)


def child_kernel(row_count, col_count, front, factor, pieces, hi, lo, work, col):
    pivots = factor.shape[1]
    factor_loop(front, factor, hi, lo, None, None, work, col, pivots // TILE, 512)
    size = pieces.shape[1]

    def piece(index, carry):
        i = index // col_count
        j = index % col_count
        a = pl.ds(pl.multiple_of(pivots + i * size, TILE), size)
        b = pl.ds(pl.multiple_of(pivots + j * size, TILE), size)
        pieces[index] = front[a, b] - product3(hi[a, :], lo[a, :], hi[b, :], lo[b, :])
        return carry

    lax.fori_loop(0, row_count * col_count, piece, 0)


def child_call(front, border, row_count, col_count):
    order = front.shape[0]
    pivots = order - border
    size = border // row_count
    return pl.pallas_call(
        functools.partial(child_kernel, row_count, col_count),
        out_shape=(
            jax.ShapeDtypeStruct((order, pivots), F32),
            jax.ShapeDtypeStruct((row_count * col_count, size, size), F32),
        ),
        in_specs=[VMEM],
        out_specs=(VMEM, VMEM),
        scratch_shapes=[
            pltpu.VMEM((order, pivots), BF16),
            pltpu.VMEM((order, pivots), BF16),
            pltpu.VMEM((TILE, 2 * TILE), F32),
            pltpu.VMEM((order, TILE), F32),
        ],
        compiler_params=PARAMS,
        name="child",
    )(front)


def reorder_kernel(order, source, target):
    target[...] = source[...]


def reorder_call(order, pieces):
    shape = (1,) + pieces.shape[1:]
    return pl.pallas_call(
        reorder_kernel,
        out_shape=jax.ShapeDtypeStruct(pieces.shape, F32),
        grid_spec=pltpu.PrefetchScalarGridSpec(
            num_scalar_prefetch=1,
            grid=(pieces.shape[0],),
            in_specs=[pl.BlockSpec(shape, lambda i, order: (order[i], 0, 0))],
            out_specs=pl.BlockSpec(shape, lambda i, order: (i, 0, 0)),
        ),
        name="reorder",
    )(order, pieces)


def assemble_kernel(row_tiles, col_tiles, block, pieces, out):
    out[...] = block[...]
    per_block = row_tiles.shape[1]

    def add(index, carry):
        for i in range(per_block):
            for j in range(per_block):
                r = pl.ds(pl.multiple_of(row_tiles[index, i] * TILE, TILE), TILE)
                c = pl.ds(pl.multiple_of(col_tiles[index, j] * TILE, TILE), TILE)
                tile = pieces[index, i * TILE : (i + 1) * TILE, j * TILE : (j + 1) * TILE]
                out[r, c] = out[r, c] + tile
        return carry

    lax.fori_loop(0, pieces.shape[0], add, 0)


def assemble_call(row_tiles, col_tiles, block, pieces):
    return pl.pallas_call(
        assemble_kernel,
        out_shape=jax.ShapeDtypeStruct(block.shape, F32),
        in_specs=[SMEM, SMEM, VMEM, VMEM],
        out_specs=VMEM,
        compiler_params=PARAMS,
        name="assemble",
    )(row_tiles, col_tiles, block, pieces)


def corner_kernel(src, out, hi, lo, inv_hi, inv_lo, work, col):
    factor_loop(
        src, out, hi, lo, inv_hi, inv_lo, work, col, src.shape[1] // TILE, src.shape[0] // 2
    )


def corner_call(src):
    order = src.shape[0]
    blocks = order // TILE
    return pl.pallas_call(
        corner_kernel,
        out_shape=(
            jax.ShapeDtypeStruct((order, order), F32),
            jax.ShapeDtypeStruct((order, order), BF16),
            jax.ShapeDtypeStruct((order, order), BF16),
            jax.ShapeDtypeStruct((blocks, TILE, TILE), BF16),
            jax.ShapeDtypeStruct((blocks, TILE, TILE), BF16),
        ),
        in_specs=[VMEM],
        out_specs=(VMEM,) * 5,
        scratch_shapes=[pltpu.VMEM((TILE, 2 * TILE), F32), pltpu.VMEM((order, TILE), F32)],
        compiler_params=PARAMS,
        name="corner",
    )(src)


def finish_kernel(place, block, left, top, corner, hi, lo, inv_hi, inv_lo, out, panel, p_hi, p_lo):
    order = block.shape[0]
    count = order // TILE
    half = order // 2

    def turn(k, carry):
        here = pl.ds(pl.multiple_of(k * TILE, TILE), TILE)
        panel[:order, here] = left[:, here]
        for m in range(count):
            panel[order + m * TILE : order + (m + 1) * TILE, here] = top[
                here, m * TILE : (m + 1) * TILE
            ].T
        return carry

    lax.fori_loop(0, count, turn, 0)

    def step(k, carry):
        here = pl.ds(pl.multiple_of(k * TILE, TILE), TILE)

        def earlier(m, carry):
            there = pl.ds(pl.multiple_of(m * TILE, TILE), TILE)
            weight = weights(hi[here, there], lo[here, there])
            for first in range(0, 2 * order, half):
                part = pl.ds(first, half)
                change = product(p_hi[part, there], p_lo[part, there], weight)
                panel[part, here] = panel[part, here] - change
            return carry

        lax.fori_loop(0, k, earlier, 0)
        weight = weights(inv_hi[k], inv_lo[k])
        for first in range(0, 2 * order, half):
            part = pl.ds(first, half)
            a_hi, a_lo = split(panel[part, here])
            solved = product(a_hi, a_lo, weight)
            panel[part, here] = solved
            s_hi, s_lo = split(solved)
            p_hi[part, here] = s_hi
            p_lo[part, here] = s_lo
        return carry

    lax.fori_loop(0, count, step, 0)
    row = place[0]
    column = place[1]

    @pl.when((row == 0) & (column == 0))
    def _():
        out[...] = corner[...]

    @pl.when((row > 0) & (column == 0))
    def _():
        out[...] = panel[:order, :]

    @pl.when((row == 0) & (column > 0))
    def _():
        def back(k, carry):
            here = pl.ds(pl.multiple_of(k * TILE, TILE), TILE)
            for m in range(count):
                out[here, m * TILE : (m + 1) * TILE] = panel[
                    order + m * TILE : order + (m + 1) * TILE, here
                ].T
            return carry

        lax.fori_loop(0, count, back, 0)

    @pl.when((row > 0) & (column > 0))
    def _():
        size = 2 * TILE
        across = order // size

        def trail(index, carry):
            i = index // across
            j = index % across
            a = pl.ds(pl.multiple_of(i * size, size), size)
            b = pl.ds(pl.multiple_of(j * size, size), size)
            c = pl.ds(pl.multiple_of(order + j * size, size), size)
            out[a, b] = block[a, b] - product3(p_hi[a, :], p_lo[a, :], p_hi[c, :], p_lo[c, :])
            return carry

        lax.fori_loop(0, across * across, trail, 0)


def finish_call(place, block, left, top, corner, hi, lo, inv_hi, inv_lo):
    order = block.shape[0]
    return pl.pallas_call(
        finish_kernel,
        out_shape=jax.ShapeDtypeStruct(block.shape, F32),
        in_specs=[SMEM] + [VMEM] * 8,
        out_specs=VMEM,
        scratch_shapes=[
            pltpu.VMEM((2 * order, order), F32),
            pltpu.VMEM((2 * order, order), BF16),
            pltpu.VMEM((2 * order, order), BF16),
        ],
        compiler_params=PARAMS,
        name="finish",
    )(place, block, left, top, corner, hi, lo, inv_hi, inv_lo)


def broadcast(array, axis, root):
    mine = lax.axis_index(axis) == root
    return lax.psum(jnp.where(mine, array, jnp.zeros_like(array)), axis)


def local(child_fronts, parent_entries, tile_map, parent_group):
    border_tiles = tile_map.shape[1]
    border = border_tiles * TILE
    row_count = lax.axis_size("row")
    col_count = lax.axis_size("col")
    front_count = lax.axis_size("front")
    row_here = lax.axis_index("row")
    col_here = lax.axis_index("col")
    front_here = lax.axis_index("front")
    group_size = row_count * col_count

    labels = jnp.concatenate([tile_map, parent_group[:, None]], 1)
    labels = lax.all_gather(labels, ("front", "row", "col"), axis=0, tiled=True)
    labels = labels.reshape(front_count, group_size, border_tiles + 1)
    groups = labels[:, :, border_tiles]
    number = jnp.arange(group_size, dtype=jnp.int32)
    ahead = (groups[:, None, :] < groups[:, :, None]) | (
        (groups[:, None, :] == groups[:, :, None]) & (number[None, None, :] < number[None, :, None])
    )
    rank = jnp.sum(ahead.astype(jnp.int32), 2)
    chosen = rank[:, None, :] == number[None, :, None]
    arrange = jnp.sum(jnp.where(chosen, number[None, None, :], 0), 2)
    per_parent = group_size // front_count
    ids = jnp.sum(
        jnp.where(chosen[:, :, :, None], labels[:, None, :, :border_tiles], 0), 2
    ).reshape(front_count, front_count, per_parent, border_tiles)
    ids = lax.dynamic_index_in_dim(ids, front_here, 1, False).reshape(-1, border_tiles)
    my_order = lax.dynamic_index_in_dim(arrange, front_here, 0, False)

    factor, pieces = child_call(child_fronts[0], border, row_count, col_count)
    size = border // row_count
    arrived = lax.all_to_all(pieces, ("row", "col"), split_axis=0, concat_axis=0, tiled=True)
    regrouped = reorder_call(my_order, arrived).reshape(front_count, per_parent, size, size)
    landed = lax.all_to_all(regrouped, "front", split_axis=0, concat_axis=0, tiled=True)
    landed = landed.reshape(-1, size, size)

    block = parent_entries[0]
    local_tiles = block.shape[0] // TILE
    per_block = border_tiles // row_count
    row_tiles = (
        lax.dynamic_slice_in_dim(ids, row_here * per_block, per_block, 1) - row_here * local_tiles
    )
    col_tiles = (
        lax.dynamic_slice_in_dim(ids, col_here * per_block, per_block, 1) - col_here * local_tiles
    )
    block = assemble_call(row_tiles, col_tiles, block, landed)
    diag = broadcast(block, ("row", "col"), 0)
    left = broadcast(block, "col", 0)
    top = broadcast(block, "row", 0)
    corner, hi, lo, inv_hi, inv_lo = corner_call(diag)
    place = jnp.stack([row_here, col_here]).astype(jnp.int32)
    result = finish_call(place, block, left, top, corner, hi, lo, inv_hi, inv_lo)
    return (factor[None], result[None])


def solution(mesh):
    in_specs = (
        P(("front", "row", "col"), None, None),
        P("front", "row", "col"),
        P(("front", "row", "col"), None),
        P(("front", "row", "col")),
    )
    out_specs = (P(("front", "row", "col"), None, None), P("front", "row", "col"))
    return jax.shard_map(local, mesh=mesh, in_specs=in_specs, out_specs=out_specs, check_vma=False)
```

time: 1420 us -> 670 us (0.47); the launches traced: 1390 us -> 669 us
  other arithmetic: 466 us -> 10 us
  local copies, waits for them, and re-layouts: 315 us -> 0.8 us
  blocking collectives: 0 us -> 139 us
  Pallas kernels: 0 us -> 136 us
  loops' own time: 120 us -> 0 us
  matrix products: 117 us -> 0 us
  waiting for transfers between devices: 331 us -> 357 us
    another operation x52 -> x1, other arithmetic: 384 us -> 0.6 us  [local(): place = jnp.stack([row_here, col_here]).astype(jnp.int32)]
    psum x3, waiting for transfers between devices: 115 us -> 317 us  [broadcast(): return lax.psum(jnp.where(mine, array, jnp.zeros_like(array)), axis)]
    dynamic_update_slice x64 -> x0, local copies, waits for them, and re-layouts: 182 us -> none  [add_piece(): lax.dynamic_update_slice(block, current + tile, (start_row, start_col))]
    all_gather x0 -> x1, blocking collectives: none -> 139 us  [local(): labels = lax.all_gather(labels, ('front', 'row', 'col'), axis=0, tiled=True)]
    pallas_call x0 -> x5, Pallas kernels: none -> 136 us  [the longest x1 45.4 us: corner_call(): pl.pallas_call(corner_kernel, out_shape=(jax.ShapeDtypeStruct((order, ord...]
    another operation x3 -> x0, loops' own time: 120 us -> none  [the longest x1 120 us: local(): local_block = lax.fori_loop(0, piece_count, add_piece, local_block)]
    all_to_all x1, waiting for transfers between devices: 87.7 us -> 0.01 us  [local(): lax.all_to_all(pieces, ('row', 'col'), split_axis=0, concat_axis=0, tiled...]
    another operation x57 -> x0, matrix products: 84.2 us -> none  [the longest x37 55.4 us: right_solve(): lax.linalg.triangular_solve(pivot_factor, matrix, left_side=False, lower=...]
  transfers between devices with their start and end apart: 9 -> 5, of which waited for: 5 -> 4; matrix products, arithmetic and copies ran while one was open for 41% -> 0% of each run, Pallas kernels for 0% -> 7%
where the time goes in v1:
time: 670 us; the launch traced here: 669 us
  waiting for transfers between devices  357 us (53%)
  blocking collectives  139 us (21%)
  Pallas kernels  136 us (20%)
  between operations  14.4 us (2%)
  starting transfers between devices  12.3 us (2%)
  other arithmetic  10 us (1%)
    psum x3, waiting for transfers between devices, broadcast(): return lax.psum(jnp.where(mine, array, jnp.zeros_like(array)), axis)  317 us
    all_gather x1, blocking collectives, local(): labels = lax.all_gather(labels, ('front', 'row', 'col'), axis=0, tiled=True)  139 us
    pallas_call x1, Pallas kernels, corner_call(): pl.pallas_call(corner_kernel, out_shape=(jax.ShapeDtypeStruct((order, ord...  45.4 us
    pallas_call x1, Pallas kernels, finish_call(): pl.pallas_call(finish_kernel, out_shape=jax.ShapeDtypeStruct(block.shape,...  42.3 us
    all_to_all x1, waiting for transfers between devices, local(): lax.all_to_all(regrouped, 'front', split_axis=0, concat_axis=0, tiled=True)  38.9 us
    pallas_call x1, Pallas kernels, child_call(): pl.pallas_call(functools.partial(child_kernel, row_count, col_count), out...  30.7 us
  transfers between devices with their start and end apart: 5, of which 4 were waited for; matrix products, arithmetic and copies ran while one was open for 0% of the time, Pallas kernels for 7%

profile of v1, /device:TPU:17, one launch (start us, length us, event | category | flops | bytes accessed | tf_op | source)
XLA Modules:
  0.0 669.2 jit_solution(9382230768385918958)
XLA Ops:
  7.2 30.7 %child.1 = (f32[1536,512]{1,0:T(8,128)}, f32[16,256,256]{2,1,0:T(8,128)}) custom-call(f32[1536,1536]{1,0:T(8,128)} %bitcast.23), custom_call_target="tpu_custom_call" | custom-call | tf_op jit(solution)/shard_map/child/pallas_call | solution.py:136
  37.8 0.0 copy-start
  37.8 6.6 all-to-all-start
  45.1 0.0 copy-done
  45.1 0.1 add_bitcast_fusion
  45.2 139.1 %all-gather = s32[32,1,9]{2,1,0:T(1,128)S(1)} all-gather(s32[1,1,9]{2,1,0:T(1,128)S(1)} %add_bitcast_fusion), channel_id=1, replica_groups=mesh['front'=2,'row'=4,'col'=4] {'front','row','col'}, dimensions={0}, use_global_device_ids=true | all-gather | bytes 1188 | tf_op jit(solution)/shard_map/all_gather | solution.py:342
  184.3 0.1 slice.8
  184.3 0.1 copy.26
  184.4 0.2 convert_reduce_fusion
  184.6 0.1 select_reduce_fusion.1
  184.8 0.6 fusion.order
  185.3 0.0 all-to-all-done.source
  185.3 10.8 %reorder.1 = f32[16,256,256]{2,1,0:T(8,128)} custom-call(s32[16]{0:T(128)} %fusion.order, f32[16,256,256]{2,1,0:T(8,128)} %all-to-all-done.source), custom_call_target="tpu_custom_call" | custom-call | tf_op jit(solution)/shard_map/reorder/pallas_call | solution.py:161
  196.1 5.6 all-to-all-start.1
  201.7 0.0 all-reduce.8.cloned.1.call-start
  201.8 0.1 copy.18
  201.8 0.6 select_reduce_fusion
  202.5 0.7 dynamic-slice_subtract_fusion
  203.2 38.9 %all-to-all-done.1 = f32[2,8,256,256]{3,2,1,0:T(8,128)} async-done(((f32[2,8,256,256]{3,2,1,0:T(8,128)}), f32[2,8,256,256]{3,2,1,0:T(8,128)}, u32[]{:S(2)}, u32[]{:S(2)}) %all-to-all-start.1) | async-done | bytes 4194336 | tf_op jit(solution)/shard_map/all_to_all | solution.py:363
  242.1 6.6 assemble.1.block
  248.7 7.7 %broadcast_select_fusion = (f32[1024,1024]{1,0:T(8,128)}, f32[1024,1024]{1,0:T(8,128)}, f32[1024,1024]{1,0:T(8,128)}) fusion(f32[1024,1024]{1,0:T(8,128)} %assemble.1.block, pred[]{:T(512)S(6)} %eq.41, pred[]{:T(512)S(6)} %eq.40, pred[]{:T(512)S(6)} %eq.39), kind=kLoop, calls=%fused_computation | loop fusion | flops 3145728 | bytes 16777220 | tf_op jit(solution)/shard_map/jit(_where)/select_n | solution.py:327
  256.4 0.0 all-reduce.8.cloned.1.call-update
  256.5 0.0 all-reduce.6.cloned.1.call-start
  256.5 0.7 all-reduce.6.cloned.1.call-update
  257.2 0.0 all-reduce.4.cloned.1.call-start
  257.3 0.7 all-reduce.4.cloned.1.call-update
  257.9 0.6 pad_add_fusion.place
  258.5 117.0 %all-reduce.8.cloned.1.call-done.src = f32[1024,1024]{1,0:T(8,128)} async-done(((f32[1024,1024]{1,0:T(8,128)}), f32[1024,1024]{1,0:T(8,128)}) %all-reduce.8.cloned.1.call-update) | async-done | bytes 4194320 | tf_op jit(solution)/shard_map/psum | solution.py:327
  375.5 45.4 %corner.1 = (f32[1024,1024]{1,0:T(8,128)}, bf16[1024,1024]{1,0:T(8,128)(2,1)}, bf16[1024,1024]{1,0:T(8,128)(2,1)}, bf16[8,128,128]{2,1,0:T(8,128)(2,1)}, bf16[8,128,128]{2,1,0:T(8,128)(2,1)}) custom-call(f32[1024,1024]{1,0:T(8,128)} %all-reduce.8.cloned.1.call-done.src), custom_call_target="tpu_custom_call" | custom-call | tf_op jit(solution)/shard_map/corner/pallas_call | solution.py:210
  420.9 42.8 %all-reduce.6.cloned.1.call-done.top = f32[1024,1024]{1,0:T(8,128)} async-done(((f32[1024,1024]{1,0:T(8,128)}), f32[1024,1024]{1,0:T(8,128)}) %all-reduce.6.cloned.1.call-update) | async-done | bytes 4194320 | tf_op jit(solution)/shard_map/psum | solution.py:327
  463.7 156.7 %all-reduce.4.cloned.1.call-done.left = f32[1024,1024]{1,0:T(8,128)} async-done(((f32[1024,1024]{1,0:T(8,128)}), f32[1024,1024]{1,0:T(8,128)}) %all-reduce.4.cloned.1.call-update) | async-done | bytes 4194320 | tf_op jit(solution)/shard_map/psum | solution.py:327
  620.4 42.3 %finish.1 = f32[1024,1024]{1,0:T(8,128)} custom-call(s32[2]{0:T(128)} %pad_add_fusion.place, f32[1024,1024]{1,0:T(8,128)} %assemble.1.block, f32[1024,1024]{1,0:T(8,128)} %all-reduce.4.cloned.1.call-done.left, f32[1024,1024]{1,0:T(8,128)} %all-reduce.6.cloned.1.call-done.top, f32[1024,1024]{1,0:T(8,128)} %get-tuple-element.11.corner, ...), custom_call_target="tpu_custom_call" | custom-call | tf_op jit(solution)/shard_map/finish/pallas_call | solution.py:310
  (3 shorter events, 0.0 us)
Async XLA Ops:
  37.8 7.3 %copy-start = (s32[1,8]{1,0:T(1,128)S(1)}, s32[1,8]{1,0:T(1,128)}, u32[]{:S(2)}) copy-start(s32[1,8]{1,0:T(1,128)} %param.6) | copy-start | bytes 100
  37.8 147.5 %all-to-all-start = ((f32[16,256,256]{2,1,0:T(8,128)}), f32[16,256,256]{2,1,0:T(8,128)}, u32[]{:S(2)}, u32[]{:S(2)}) async-start(f32[16,256,256]{2,1,0:T(8,128)} %get-tuple-element.10), calls=%async_computation | async-start | bytes 8388608 | tf_op jit(solution)/shard_map/all_to_all | solution.py:361
  196.1 46.0 %all-to-all-start.1 = ((f32[2,8,256,256]{3,2,1,0:T(8,128)}), f32[2,8,256,256]{3,2,1,0:T(8,128)}, u32[]{:S(2)}, u32[]{:S(2)}) async-start(f32[2,8,256,256]{3,2,1,0:T(8,128)} %bitcast.22), calls=%async_computation.1 | async-start | bytes 8388608 | tf_op jit(solution)/shard_map/all_to_all | solution.py:363
  201.7 173.8 %all-reduce.8.cloned.1.call-start = ((), (), s32[]{:S(2)}) async-start(), calls=%async_computation.4 | async-start | bytes 8388608 | tf_op jit(solution)/shard_map/psum | solution.py:327
  256.5 207.3 %all-reduce.6.cloned.1.call-start = ((), (), s32[]{:S(2)}) async-start(), calls=%async_computation.3 | async-start | bytes 8388608 | tf_op jit(solution)/shard_map/psum | solution.py:327
  257.2 363.2 %all-reduce.4.cloned.1.call-start = ((), (), s32[]{:S(2)}) async-start(), calls=%async_computation.2 | async-start | bytes 8388608 | tf_op jit(solution)/shard_map/psum | solution.py:327
Sparse Core Ops, SparseCore 0:
  256.6 118.9 all-reduce.7
  378.0 85.6 all-reduce.5
  466.1 154.2 all-reduce.3

commit v2 on v1

--- a/solution.py
+++ b/solution.py
@@ -171,7 +171,7 @@
     )(order, pieces)
 
 
-def assemble_kernel(row_tiles, col_tiles, block, pieces, out):
+def assemble_kernel(place, row_tiles, col_tiles, block, pieces, out, turned):
     out[...] = block[...]
     per_block = row_tiles.shape[1]
 
@@ -185,17 +185,30 @@
         return carry
 
     lax.fori_loop(0, pieces.shape[0], add, 0)
-
-
-def assemble_call(row_tiles, col_tiles, block, pieces):
+    turned[...] = jnp.zeros_like(turned)
+
+    @pl.when(place[0] == 0)
+    def _():
+        count = out.shape[0] // TILE
+
+        def turn(k, carry):
+            here = pl.ds(pl.multiple_of(k * TILE, TILE), TILE)
+            for m in range(count):
+                turned[m * TILE : (m + 1) * TILE, here] = out[here, m * TILE : (m + 1) * TILE].T
+            return carry
+
+        lax.fori_loop(0, count, turn, 0)
+
+
+def assemble_call(place, row_tiles, col_tiles, block, pieces):
     return pl.pallas_call(
         assemble_kernel,
-        out_shape=jax.ShapeDtypeStruct(block.shape, F32),
-        in_specs=[SMEM, SMEM, VMEM, VMEM],
-        out_specs=VMEM,
+        out_shape=(jax.ShapeDtypeStruct(block.shape, F32),) * 2,
+        in_specs=[SMEM, SMEM, SMEM, VMEM, VMEM],
+        out_specs=(VMEM, VMEM),
         compiler_params=PARAMS,
         name="assemble",
-    )(row_tiles, col_tiles, block, pieces)
+    )(place, row_tiles, col_tiles, block, pieces)
 
 
 def corner_kernel(src, out, hi, lo, inv_hi, inv_lo, work, col):
@@ -224,21 +237,11 @@
     )(src)
 
 
-def finish_kernel(place, block, left, top, corner, hi, lo, inv_hi, inv_lo, out, panel, p_hi, p_lo):
-    order = block.shape[0]
-    count = order // TILE
-    half = order // 2
-
-    def turn(k, carry):
-        here = pl.ds(pl.multiple_of(k * TILE, TILE), TILE)
-        panel[:order, here] = left[:, here]
-        for m in range(count):
-            panel[order + m * TILE : order + (m + 1) * TILE, here] = top[
-                here, m * TILE : (m + 1) * TILE
-            ].T
-        return carry
-
-    lax.fori_loop(0, count, turn, 0)
+def solve_kernel(left, top, hi, lo, inv_hi, inv_lo, panel, p_hi, p_lo):
+    count = hi.shape[0] // TILE
+    share = left.shape[0]
+    panel[:share, :] = left[...]
+    panel[share:, :] = top[...]
 
     def step(k, carry):
         here = pl.ds(pl.multiple_of(k * TILE, TILE), TILE)
@@ -246,25 +249,116 @@
         def earlier(m, carry):
             there = pl.ds(pl.multiple_of(m * TILE, TILE), TILE)
             weight = weights(hi[here, there], lo[here, there])
-            for first in range(0, 2 * order, half):
-                part = pl.ds(first, half)
-                change = product(p_hi[part, there], p_lo[part, there], weight)
-                panel[part, here] = panel[part, here] - change
+            panel[:, here] = panel[:, here] - product(p_hi[:, there], p_lo[:, there], weight)
             return carry
 
         lax.fori_loop(0, k, earlier, 0)
-        weight = weights(inv_hi[k], inv_lo[k])
-        for first in range(0, 2 * order, half):
-            part = pl.ds(first, half)
-            a_hi, a_lo = split(panel[part, here])
-            solved = product(a_hi, a_lo, weight)
-            panel[part, here] = solved
-            s_hi, s_lo = split(solved)
-            p_hi[part, here] = s_hi
-            p_lo[part, here] = s_lo
+        a_hi, a_lo = split(panel[:, here])
+        solved = product(a_hi, a_lo, weights(inv_hi[k], inv_lo[k]))
+        panel[:, here] = solved
+        s_hi, s_lo = split(solved)
+        p_hi[:, here] = s_hi
+        p_lo[:, here] = s_lo
         return carry
 
     lax.fori_loop(0, count, step, 0)
+
+
+def solve_call(left, top, hi, lo, inv_hi, inv_lo):
+    shape = (left.shape[0] + top.shape[0], left.shape[1])
+    return pl.pallas_call(
+        solve_kernel,
+        out_shape=jax.ShapeDtypeStruct(shape, F32),
+        in_specs=[VMEM] * 6,
+        out_specs=VMEM,
+        scratch_shapes=[pltpu.VMEM(shape, BF16), pltpu.VMEM(shape, BF16)],
+        compiler_params=PARAMS,
+        name="solve",
+    )(left, top, hi, lo, inv_hi, inv_lo)
+
+
+def gather_kernel(rows, cols, part, row_out, col_out, own, send_row, get_row, send_col, get_col):
+    row = lax.axis_index("row")
+    column = lax.axis_index("col")
+    share = part.shape[0] - row_out.shape[0] // cols
+    first = part.shape[0] - share
+    barrier = pltpu.get_barrier_semaphore()
+    for step in range(1, cols):
+        peer = {"col": lax.rem(column + step, cols)}
+        pl.semaphore_signal(barrier, inc=1, device_id=peer, device_id_type=pl.DeviceIdType.MESH)
+    for step in range(1, rows):
+        peer = {"row": lax.rem(row + step, rows)}
+        pl.semaphore_signal(barrier, inc=1, device_id=peer, device_id_type=pl.DeviceIdType.MESH)
+    pl.semaphore_wait(barrier, cols + rows - 2)
+    copies = []
+    for step in range(1, cols):
+        copies.append(
+            pltpu.make_async_remote_copy(
+                src_ref=part.at[pl.ds(0, first)],
+                dst_ref=row_out.at[pl.ds(pl.multiple_of(column * first, first), first)],
+                send_sem=send_row.at[step - 1],
+                recv_sem=get_row.at[step - 1],
+                device_id={"col": lax.rem(column + step, cols)},
+                device_id_type=pl.DeviceIdType.MESH,
+            )
+        )
+    for step in range(1, rows):
+        copies.append(
+            pltpu.make_async_remote_copy(
+                src_ref=part.at[pl.ds(first, share)],
+                dst_ref=col_out.at[pl.ds(pl.multiple_of(row * share, share), share)],
+                send_sem=send_col.at[step - 1],
+                recv_sem=get_col.at[step - 1],
+                device_id={"row": lax.rem(row + step, rows)},
+                device_id_type=pl.DeviceIdType.MESH,
+            )
+        )
+    for copy in copies:
+        copy.start()
+    mine = (
+        pltpu.make_async_copy(
+            part.at[pl.ds(0, first)],
+            row_out.at[pl.ds(pl.multiple_of(column * first, first), first)],
+            own.at[0],
+        ),
+        pltpu.make_async_copy(
+            part.at[pl.ds(first, share)],
+            col_out.at[pl.ds(pl.multiple_of(row * share, share), share)],
+            own.at[1],
+        ),
+    )
+    for copy in mine:
+        copy.start()
+    for copy in mine:
+        copy.wait()
+    for copy in copies:
+        copy.wait()
+
+
+def gather_call(part, order, rows, cols):
+    anywhere = pl.BlockSpec(memory_space=pl.ANY)
+    return pl.pallas_call(
+        functools.partial(gather_kernel, rows, cols),
+        out_shape=(jax.ShapeDtypeStruct((order, order), F32),) * 2,
+        in_specs=[anywhere],
+        out_specs=(anywhere, anywhere),
+        scratch_shapes=[
+            pltpu.SemaphoreType.DMA((2,)),
+            pltpu.SemaphoreType.DMA((cols - 1,)),
+            pltpu.SemaphoreType.DMA((cols - 1,)),
+            pltpu.SemaphoreType.DMA((rows - 1,)),
+            pltpu.SemaphoreType.DMA((rows - 1,)),
+        ],
+        compiler_params=pltpu.CompilerParams(
+            collective_id=1, has_side_effects=True, vmem_limit_bytes=32 * 1024 * 1024
+        ),
+        name="gather",
+    )(part)
+
+
+def finish_kernel(place, block, across, down, corner, out):
+    order = block.shape[0]
+    count = order // TILE
     row = place[0]
     column = place[1]
 
@@ -274,16 +368,14 @@
 
     @pl.when((row > 0) & (column == 0))
     def _():
-        out[...] = panel[:order, :]
+        out[...] = across[...]
 
     @pl.when((row == 0) & (column > 0))
     def _():
         def back(k, carry):
             here = pl.ds(pl.multiple_of(k * TILE, TILE), TILE)
             for m in range(count):
-                out[here, m * TILE : (m + 1) * TILE] = panel[
-                    order + m * TILE : order + (m + 1) * TILE, here
-                ].T
+                out[here, m * TILE : (m + 1) * TILE] = down[m * TILE : (m + 1) * TILE, here].T
             return carry
 
         lax.fori_loop(0, count, back, 0)
@@ -291,35 +383,28 @@
     @pl.when((row > 0) & (column > 0))
     def _():
         size = 2 * TILE
-        across = order // size
+        wide = order // size
 
         def trail(index, carry):
-            i = index // across
-            j = index % across
-            a = pl.ds(pl.multiple_of(i * size, size), size)
-            b = pl.ds(pl.multiple_of(j * size, size), size)
-            c = pl.ds(pl.multiple_of(order + j * size, size), size)
-            out[a, b] = block[a, b] - product3(p_hi[a, :], p_lo[a, :], p_hi[c, :], p_lo[c, :])
+            a = pl.ds(pl.multiple_of(index // wide * size, size), size)
+            b = pl.ds(pl.multiple_of(index % wide * size, size), size)
+            a_hi, a_lo = split(across[a, :])
+            b_hi, b_lo = split(down[b, :])
+            out[a, b] = block[a, b] - product3(a_hi, a_lo, b_hi, b_lo)
             return carry
 
-        lax.fori_loop(0, across * across, trail, 0)
-
-
-def finish_call(place, block, left, top, corner, hi, lo, inv_hi, inv_lo):
-    order = block.shape[0]
+        lax.fori_loop(0, wide * wide, trail, 0)
+
+
+def finish_call(place, block, across, down, corner):
     return pl.pallas_call(
         finish_kernel,
         out_shape=jax.ShapeDtypeStruct(block.shape, F32),
-        in_specs=[SMEM] + [VMEM] * 8,
+        in_specs=[SMEM] + [VMEM] * 4,
         out_specs=VMEM,
-        scratch_shapes=[
-            pltpu.VMEM((2 * order, order), F32),
-            pltpu.VMEM((2 * order, order), BF16),
-            pltpu.VMEM((2 * order, order), BF16),
-        ],
         compiler_params=PARAMS,
         name="finish",
-    )(place, block, left, top, corner, hi, lo, inv_hi, inv_lo)
+    )(place, block, across, down, corner)
 
 
 def broadcast(array, axis, root):
@@ -356,7 +441,8 @@
     ids = lax.dynamic_index_in_dim(ids, front_here, 1, False).reshape(-1, border_tiles)
     my_order = lax.dynamic_index_in_dim(arrange, front_here, 0, False)
 
-    factor, pieces = child_call(child_fronts[0], border, row_count, col_count)
+    child, ids, my_order = lax.optimization_barrier((child_fronts[0], ids, my_order))
+    factor, pieces = child_call(child, border, row_count, col_count)
     size = border // row_count
     arrived = lax.all_to_all(pieces, ("row", "col"), split_axis=0, concat_axis=0, tiled=True)
     regrouped = reorder_call(my_order, arrived).reshape(front_count, per_parent, size, size)
@@ -372,13 +458,18 @@
     col_tiles = (
         lax.dynamic_slice_in_dim(ids, col_here * per_block, per_block, 1) - col_here * local_tiles
     )
-    block = assemble_call(row_tiles, col_tiles, block, landed)
+    place = jnp.stack([row_here, col_here]).astype(jnp.int32)
+    block, turned = assemble_call(place, row_tiles, col_tiles, block, landed)
+    order = block.shape[0]
     diag = broadcast(block, ("row", "col"), 0)
-    left = broadcast(block, "col", 0)
-    top = broadcast(block, "row", 0)
+    left = block.reshape(col_count, order // col_count, order)
+    left = lax.all_to_all(left, "col", split_axis=0, concat_axis=0, tiled=True)
+    top = turned.reshape(row_count, order // row_count, order)
+    top = lax.all_to_all(top, "row", split_axis=0, concat_axis=0, tiled=True)
     corner, hi, lo, inv_hi, inv_lo = corner_call(diag)
-    place = jnp.stack([row_here, col_here]).astype(jnp.int32)
-    result = finish_call(place, block, left, top, corner, hi, lo, inv_hi, inv_lo)
+    part = solve_call(left[0], top[0], hi, lo, inv_hi, inv_lo)
+    across, down = gather_call(part, order, row_count, col_count)
+    result = finish_call(place, block, across, down, corner)
     return (factor[None], result[None])
 
 

time: 670 us -> 719 us (1.073)
  waiting for transfers between devices: 357 us -> 232 us
  Pallas kernels: 136 us -> 220 us
  blocking collectives: 139 us -> 220 us
  local copies, waits for them, and re-layouts: 0.8 us -> 11 us
    all_to_all x0 -> x2, blocking collectives: none -> 162 us  [the longest x1 107 us: local(): lax.all_to_all(pieces, ('row', 'col'), split_axis=0, concat_axis=0, tiled...]
    psum x3 -> x1, waiting for transfers between devices: 317 us -> 186 us  [broadcast(): return lax.psum(jnp.where(mine, array, jnp.zeros_like(array)), axis)]
    pallas_call x1 -> x3, Pallas kernels: 6.58 us -> 115 us  [the longest x1 92.3 us: gather_call(): pl.pallas_call(functools.partial(gather_kernel, rows, cols), out_shape=(j...]
    all_gather x1, blocking collectives: 139 us -> 57.7 us  [local(): labels = lax.all_gather(labels, ('front', 'row', 'col'), axis=0, tiled=True)]
    pallas_call x1, Pallas kernels: 42.3 us -> 18 us  [finish_call(): pl.pallas_call(finish_kernel, out_shape=jax.ShapeDtypeStruct(block.shape,...]
    all_to_all x1, waiting for transfers between devices: 38.9 us -> 46.2 us  [local(): lax.all_to_all(regrouped, 'front', split_axis=0, concat_axis=0, tiled=True)]
  transfers between devices with their start and end apart: 5 -> 3, of which waited for: 4 -> 2; matrix products, arithmetic and copies ran while one was open for 0% -> 1% of each run, Pallas kernels for 7% -> 6%
where the time goes in v2:
time: 719 us; the launch traced here: 716 us
  waiting for transfers between devices  232 us (32%)
  blocking collectives  220 us (31%)
  Pallas kernels  220 us (31%)
  between operations  14.7 us (2%)
  starting transfers between devices  12.6 us (2%)
  local copies, waits for them, and re-layouts  11 us (2%)
    psum x1, waiting for transfers between devices, broadcast(): return lax.psum(jnp.where(mine, array, jnp.zeros_like(array)), axis)  186 us
    all_to_all x1, blocking collectives, local(): lax.all_to_all(pieces, ('row', 'col'), split_axis=0, concat_axis=0, tiled...  107 us
    pallas_call x1, Pallas kernels, gather_call(): pl.pallas_call(functools.partial(gather_kernel, rows, cols), out_shape=(j...  92.3 us
    all_gather x1, blocking collectives, local(): labels = lax.all_gather(labels, ('front', 'row', 'col'), axis=0, tiled=True)  57.7 us
    all_to_all x1, blocking collectives, local(): top = lax.all_to_all(top, 'row', split_axis=0, concat_axis=0, tiled=True)  55.2 us
    all_to_all x1, waiting for transfers between devices, local(): lax.all_to_all(regrouped, 'front', split_axis=0, concat_axis=0, tiled=True)  46.2 us
    pallas_call x1, Pallas kernels, corner_call(): pl.pallas_call(corner_kernel, out_shape=(jax.ShapeDtypeStruct((order, ord...  45.5 us
    pallas_call x1, Pallas kernels, child_call(): pl.pallas_call(functools.partial(child_kernel, row_count, col_count), out...  30.7 us
  transfers between devices with their start and end apart: 3, of which 2 were waited for; matrix products, arithmetic and copies ran while one was open for 1% of the time, Pallas kernels for 6%

profile of v2, /device:TPU:17, one launch (start us, length us, event | category | flops | bytes accessed | tf_op | source)
XLA Modules:
  0.0 715.6 jit_solution(8380739253296652037)
XLA Ops:
  7.8 0.7 add_bitcast_fusion
  8.6 57.7 %all-gather = s32[32,1,9]{2,1,0:T(1,128)S(1)} all-gather(s32[1,1,9]{2,1,0:T(1,128)S(1)} %add_bitcast_fusion), channel_id=1, replica_groups=mesh['front'=2,'row'=4,'col'=4] {'front','row','col'}, dimensions={0}, use_global_device_ids=true | all-gather | bytes 1188 | tf_op jit(solution)/shard_map/all_gather | solution.py:427
  66.2 0.1 slice.16
  66.3 0.1 copy.24
  66.4 0.2 convert_reduce_fusion
  66.6 0.1 select_reduce_fusion.1
  66.7 0.1 copy.18
  66.8 0.5 fusion.order
  67.3 0.6 select_reduce_fusion
  67.9 0.1 copy.27
  68.0 30.7 %child.1 = (f32[1536,512]{1,0:T(8,128)}, f32[16,256,256]{2,1,0:T(8,128)}) custom-call(f32[1536,1536]{1,0:T(8,128)} %bitcast.28), custom_call_target="tpu_custom_call" | custom-call | tf_op jit(solution)/shard_map/child/pallas_call | solution.py:136
  98.7 106.9 %all_to_all.20.source = f32[16,256,256]{2,1,0:T(8,128)} all-to-all(f32[16,256,256]{2,1,0:T(8,128)} %get-tuple-element.20), channel_id=1, replica_groups=mesh['front'=2,'row'=4,'col'=4] {'row','col'}, dimensions={0} | all-to-all | bytes 8388608 | tf_op jit(solution)/shard_map/all_to_all | solution.py:447
  205.6 10.8 %reorder.1 = f32[16,256,256]{2,1,0:T(8,128)} custom-call(s32[16]{0:T(128)} %fusion.order, f32[16,256,256]{2,1,0:T(8,128)} %all_to_all.20.source), custom_call_target="tpu_custom_call" | custom-call | tf_op jit(solution)/shard_map/reorder/pallas_call | solution.py:161
  216.4 5.6 all-to-all-start.1
  222.0 0.1 copy.21
  222.0 0.6 pad_add_fusion.place
  222.6 0.7 dynamic-slice_subtract_fusion
  223.3 46.2 %all-to-all-done.1 = f32[2,8,256,256]{3,2,1,0:T(8,128)} async-done(((f32[2,8,256,256]{3,2,1,0:T(8,128)}), f32[2,8,256,256]{3,2,1,0:T(8,128)}, u32[]{:S(2)}, u32[]{:S(2)}) %all-to-all-start.1) | async-done | bytes 4194336 | tf_op jit(solution)/shard_map/all_to_all | solution.py:449
  269.5 8.3 %assemble.1 = (f32[1024,1024]{1,0:T(8,128)}, f32[1024,1024]{1,0:T(8,128)}) custom-call(s32[2]{0:T(128)} %pad_add_fusion.place, s32[16,2]{1,0:T(8,128)} %get-tuple-element.31.row_tiles, s32[16,2]{1,0:T(8,128)} %get-tuple-element.30.col_tiles, f32[1024,1024]{1,0:T(8,128)} %bitcast.29, f32[16,256,256]{2,1,0:T(8,128)} %bitcast.12.pieces), custom_call_target="tpu_custom_call" | custom-call | tf_op jit(solution)/shard_map/assemble/pallas_call | solution.py:204
  277.8 55.2 %all_to_all.21 = f32[4,256,1024]{2,1,0:T(8,128)} all-to-all(f32[4,256,1024]{2,1,0:T(8,128)} %bitcast.30), channel_id=1, replica_groups=mesh['front'=2,'row'=4,'col'=4] {'row'}, dimensions={0} | all-to-all | bytes 8388608 | tf_op jit(solution)/shard_map/all_to_all | solution.py:468
  333.0 7.0 all-to-all-start.2
  340.0 0.0 all-reduce.2.cloned.1.call-start
  340.0 2.8 broadcast_select_fusion
  342.8 0.0 all-reduce.2.cloned.1.call-update
  342.9 185.7 %all-reduce.2.cloned.1.call-done.src = f32[1024,1024]{1,0:T(8,128)} async-done(((f32[1024,1024]{1,0:T(8,128)}), f32[1024,1024]{1,0:T(8,128)}) %all-reduce.2.cloned.1.call-update) | async-done | bytes 4194320 | tf_op jit(solution)/shard_map/psum | solution.py:412
  528.5 45.5 %corner.1 = (f32[1024,1024]{1,0:T(8,128)}, bf16[1024,1024]{1,0:T(8,128)(2,1)}, bf16[1024,1024]{1,0:T(8,128)(2,1)}, bf16[8,128,128]{2,1,0:T(8,128)(2,1)}, bf16[8,128,128]{2,1,0:T(8,128)(2,1)}) custom-call(f32[1024,1024]{1,0:T(8,128)} %all-reduce.2.cloned.1.call-done.src), custom_call_target="tpu_custom_call" | custom-call | tf_op jit(solution)/shard_map/corner/pallas_call | solution.py:223
  574.0 2.3 slice_bitcast_fusion.top
  576.3 0.0 all-to-all-done.2
  576.3 2.4 slice_bitcast_fusion.1.left
  578.7 14.2 %solve.1.part = f32[512,1024]{1,0:T(8,128)} custom-call(f32[256,1024]{1,0:T(8,128)} %slice_bitcast_fusion.1.left, f32[256,1024]{1,0:T(8,128)} %slice_bitcast_fusion.top, bf16[1024,1024]{1,0:T(8,128)(2,1)} %get-tuple-element.23.hi, bf16[1024,1024]{1,0:T(8,128)(2,1)} %get-tuple-element.24.lo, bf16[8,128,128]{2,1,0:T(8,128)(2,1)} %get-tuple-element.25.inv_hi, ...), custom_call_target="tpu_custom_call" | custom-call | tf_op jit(solution)/shard_map/solve/pallas_call | solution.py:269
  592.9 0.0 copy-start
  592.9 1.6 copy-done
  594.4 92.3 %gather.1 = (f32[1024,1024]{1,0:T(8,128)S(1)}, f32[1024,1024]{1,0:T(8,128)S(1)}) custom-call(f32[512,1024]{1,0:T(8,128)S(1)} %copy-done), custom_call_target="tpu_custom_call" | custom-call | tf_op jit(solution)/shard_map/gather/pallas_call | solution.py:340
  686.8 0.0 copy-start.1
  686.8 1.9 copy-done.1
  688.7 0.0 copy-start.2
  688.7 1.9 copy-done.2
  690.7 18.0 %finish.1 = f32[1024,1024]{1,0:T(8,128)} custom-call(s32[2]{0:T(128)} %pad_add_fusion.place, f32[1024,1024]{1,0:T(8,128)} %get-tuple-element.21.block, f32[1024,1024]{1,0:T(8,128)} %copy-done.1, f32[1024,1024]{1,0:T(8,128)} %copy-done.2, f32[1024,1024]{1,0:T(8,128)} %get-tuple-element.29.corner), custom_call_target="tpu_custom_call" | custom-call | tf_op jit(solution)/shard_map/finish/pallas_call | solution.py:400
  (3 shorter events, 0.0 us)
Async XLA Ops:
  216.4 53.2 %all-to-all-start.1 = ((f32[2,8,256,256]{3,2,1,0:T(8,128)}), f32[2,8,256,256]{3,2,1,0:T(8,128)}, u32[]{:S(2)}, u32[]{:S(2)}) async-start(f32[2,8,256,256]{3,2,1,0:T(8,128)} %bitcast.27), calls=%async_computation.1 | async-start | bytes 8388608 | tf_op jit(solution)/shard_map/all_to_all | solution.py:449
  333.0 243.3 %all-to-all-start.2 = ((f32[4,256,1024]{2,1,0:T(8,128)}), f32[4,256,1024]{2,1,0:T(8,128)}, u32[]{:S(2)}, u32[]{:S(2)}) async-start(f32[4,256,1024]{2,1,0:T(8,128)} %bitcast.26), calls=%async_computation.2 | async-start | bytes 8388608 | tf_op jit(solution)/shard_map/all_to_all | solution.py:466
  340.0 188.5 %all-reduce.2.cloned.1.call-start = ((), (), s32[]{:S(2)}) async-start(), calls=%async_computation.4 | async-start | bytes 8388608 | tf_op jit(solution)/shard_map/psum | solution.py:412
  592.9 1.6 copy-start
  686.8 1.9 copy-start.1
  688.7 1.9 copy-start.2
Sparse Core Ops, SparseCore 0:
  345.1 183.4 all-reduce.1

commit v3 on v2

--- a/solution.py
+++ b/solution.py
@@ -441,8 +441,7 @@
     ids = lax.dynamic_index_in_dim(ids, front_here, 1, False).reshape(-1, border_tiles)
     my_order = lax.dynamic_index_in_dim(arrange, front_here, 0, False)
 
-    child, ids, my_order = lax.optimization_barrier((child_fronts[0], ids, my_order))
-    factor, pieces = child_call(child, border, row_count, col_count)
+    factor, pieces = child_call(child_fronts[0], border, row_count, col_count)
     size = border // row_count
     arrived = lax.all_to_all(pieces, ("row", "col"), split_axis=0, concat_axis=0, tiled=True)
     regrouped = reorder_call(my_order, arrived).reshape(front_count, per_parent, size, size)
@@ -462,6 +461,7 @@
     block, turned = assemble_call(place, row_tiles, col_tiles, block, landed)
     order = block.shape[0]
     diag = broadcast(block, ("row", "col"), 0)
+    diag, block, turned = lax.optimization_barrier((diag, block, turned))
     left = block.reshape(col_count, order // col_count, order)
     left = lax.all_to_all(left, "col", split_axis=0, concat_axis=0, tiled=True)
     top = turned.reshape(row_count, order // row_count, order)

time: 719 us -> 668 us (0.929)
  waiting for transfers between devices: 232 us -> 203 us
  blocking collectives: 220 us -> 193 us
    all_to_all x1 -> x0, blocking collectives: 107 us -> none  [local(): lax.all_to_all(pieces, ('row', 'col'), split_axis=0, concat_axis=0, tiled...]
    all_gather x1, blocking collectives: 57.7 us -> 139 us  [local(): labels = lax.all_gather(labels, ('front', 'row', 'col'), axis=0, tiled=True)]
    psum x1, waiting for transfers between devices: 186 us -> 123 us  [broadcast(): return lax.psum(jnp.where(mine, array, jnp.zeros_like(array)), axis)]
    all_to_all x1, waiting for transfers between devices: 0.01 us -> 41.8 us  [local(): left = lax.all_to_all(left, 'col', split_axis=0, concat_axis=0, tiled=True)]
    all_to_all x1, waiting for transfers between devices: 46.2 us -> 38.3 us  [local(): lax.all_to_all(regrouped, 'front', split_axis=0, concat_axis=0, tiled=True)]
  transfers between devices with their start and end apart: 3 -> 4, of which waited for: 2 -> 3; matrix products, arithmetic and copies ran while one was open for 1% -> 1% of each run, Pallas kernels for 6% -> 7%
where the time goes in v3:
time: 668 us; the launch traced here: 665 us
  Pallas kernels  220 us (33%)
  waiting for transfers between devices  203 us (30%)
  blocking collectives  193 us (29%)
  starting transfers between devices  18.3 us (3%)
  between operations  14.7 us (2%)
  local copies, waits for them, and re-layouts  11 us (2%)
    all_gather x1, blocking collectives, local(): labels = lax.all_gather(labels, ('front', 'row', 'col'), axis=0, tiled=True)  139 us
    psum x1, waiting for transfers between devices, broadcast(): return lax.psum(jnp.where(mine, array, jnp.zeros_like(array)), axis)  123 us
    pallas_call x1, Pallas kernels, gather_call(): pl.pallas_call(functools.partial(gather_kernel, rows, cols), out_shape=(j...  92.6 us
    all_to_all x1, blocking collectives, local(): top = lax.all_to_all(top, 'row', split_axis=0, concat_axis=0, tiled=True)  53.9 us
    pallas_call x1, Pallas kernels, corner_call(): pl.pallas_call(corner_kernel, out_shape=(jax.ShapeDtypeStruct((order, ord...  45.5 us
    all_to_all x1, waiting for transfers between devices, local(): left = lax.all_to_all(left, 'col', split_axis=0, concat_axis=0, tiled=True)  41.8 us
    all_to_all x1, waiting for transfers between devices, local(): lax.all_to_all(regrouped, 'front', split_axis=0, concat_axis=0, tiled=True)  38.3 us
    pallas_call x1, Pallas kernels, child_call(): pl.pallas_call(functools.partial(child_kernel, row_count, col_count), out...  30.7 us
  transfers between devices with their start and end apart: 4, of which 3 were waited for; matrix products, arithmetic and copies ran while one was open for 1% of the time, Pallas kernels for 7%

profile of v3, /device:TPU:17, one launch (start us, length us, event | category | flops | bytes accessed | tf_op | source)
XLA Modules:
  0.0 665.1 jit_solution(15368186168353228095)
XLA Ops:
  7.2 30.7 %child.1 = (f32[1536,512]{1,0:T(8,128)}, f32[16,256,256]{2,1,0:T(8,128)}) custom-call(f32[1536,1536]{1,0:T(8,128)} %bitcast.30), custom_call_target="tpu_custom_call" | custom-call | tf_op jit(solution)/shard_map/child/pallas_call | solution.py:136
  37.8 0.0 copy-start.3
  37.8 6.6 all-to-all-start
  45.1 0.0 copy-done.3
  45.1 0.1 add_bitcast_fusion
  45.2 139.1 %all-gather = s32[32,1,9]{2,1,0:T(1,128)S(1)} all-gather(s32[1,1,9]{2,1,0:T(1,128)S(1)} %add_bitcast_fusion), channel_id=1, replica_groups=mesh['front'=2,'row'=4,'col'=4] {'front','row','col'}, dimensions={0}, use_global_device_ids=true | all-gather | bytes 1188 | tf_op jit(solution)/shard_map/all_gather | solution.py:427
  184.3 0.1 slice.16
  184.3 0.1 copy.26
  184.4 0.2 convert_reduce_fusion
  184.6 0.1 select_reduce_fusion.1
  184.8 0.5 fusion.order
  185.3 0.0 all-to-all-done.source
  185.3 10.8 %reorder.1 = f32[16,256,256]{2,1,0:T(8,128)} custom-call(s32[16]{0:T(128)} %fusion.order, f32[16,256,256]{2,1,0:T(8,128)} %all-to-all-done.source), custom_call_target="tpu_custom_call" | custom-call | tf_op jit(solution)/shard_map/reorder/pallas_call | solution.py:161
  196.1 5.6 all-to-all-start.1
  201.7 0.0 all-reduce.2.cloned.1.call-start
  201.7 0.1 copy.18
  201.8 0.6 pad_add_fusion.place
  202.4 0.6 select_reduce_fusion
  203.1 0.7 dynamic-slice_subtract_fusion
  203.8 38.3 %all-to-all-done.1 = f32[2,8,256,256]{3,2,1,0:T(8,128)} async-done(((f32[2,8,256,256]{3,2,1,0:T(8,128)}), f32[2,8,256,256]{3,2,1,0:T(8,128)}, u32[]{:S(2)}, u32[]{:S(2)}) %all-to-all-start.1) | async-done | bytes 4194336 | tf_op jit(solution)/shard_map/all_to_all | solution.py:448
  242.1 8.3 %assemble.1 = (f32[1024,1024]{1,0:T(8,128)}, f32[1024,1024]{1,0:T(8,128)}) custom-call(s32[2]{0:T(128)} %pad_add_fusion.place, s32[16,2]{1,0:T(8,128)} %get-tuple-element.31.row_tiles, s32[16,2]{1,0:T(8,128)} %get-tuple-element.30.col_tiles, f32[1024,1024]{1,0:T(8,128)} %bitcast.31, f32[16,256,256]{2,1,0:T(8,128)} %bitcast.13.pieces), custom_call_target="tpu_custom_call" | custom-call | tf_op jit(solution)/shard_map/assemble/pallas_call | solution.py:204
  250.4 2.8 broadcast_select_fusion
  253.2 0.0 all-reduce.2.cloned.1.call-update
  253.2 122.8 %all-reduce.2.cloned.1.call-done.src = f32[1024,1024]{1,0:T(8,128)} async-done(((f32[1024,1024]{1,0:T(8,128)}), f32[1024,1024]{1,0:T(8,128)}) %all-reduce.2.cloned.1.call-update) | async-done | bytes 4194320 | tf_op jit(solution)/shard_map/psum | solution.py:412
  376.0 53.9 %all_to_all.20 = f32[4,256,1024]{2,1,0:T(8,128)} all-to-all(f32[4,256,1024]{2,1,0:T(8,128)} %bitcast.32), channel_id=1, replica_groups=mesh['front'=2,'row'=4,'col'=4] {'row'}, dimensions={0} | all-to-all | bytes 8388608 | tf_op jit(solution)/shard_map/all_to_all | solution.py:468
  429.8 6.1 all-to-all-start.2
  435.9 45.5 %corner.1 = (f32[1024,1024]{1,0:T(8,128)}, bf16[1024,1024]{1,0:T(8,128)(2,1)}, bf16[1024,1024]{1,0:T(8,128)(2,1)}, bf16[8,128,128]{2,1,0:T(8,128)(2,1)}, bf16[8,128,128]{2,1,0:T(8,128)(2,1)}) custom-call(f32[1024,1024]{1,0:T(8,128)} %all-reduce.2.cloned.1.call-done.src), custom_call_target="tpu_custom_call" | custom-call | tf_op jit(solution)/shard_map/corner/pallas_call | solution.py:223
  481.4 2.4 slice_bitcast_fusion.top
  483.7 41.8 %all-to-all-done.2 = f32[4,256,1024]{2,1,0:T(8,128)} async-done(((f32[4,256,1024]{2,1,0:T(8,128)}), f32[4,256,1024]{2,1,0:T(8,128)}, u32[]{:S(2)}, u32[]{:S(2)}) %all-to-all-start.2) | async-done | bytes 4194336 | tf_op jit(solution)/shard_map/all_to_all | solution.py:466
  525.5 2.3 slice_bitcast_fusion.1.left
  527.9 14.2 %solve.1.part = f32[512,1024]{1,0:T(8,128)} custom-call(f32[256,1024]{1,0:T(8,128)} %slice_bitcast_fusion.1.left, f32[256,1024]{1,0:T(8,128)} %slice_bitcast_fusion.top, bf16[1024,1024]{1,0:T(8,128)(2,1)} %get-tuple-element.23.hi, bf16[1024,1024]{1,0:T(8,128)(2,1)} %get-tuple-element.24.lo, bf16[8,128,128]{2,1,0:T(8,128)(2,1)} %get-tuple-element.25.inv_hi, ...), custom_call_target="tpu_custom_call" | custom-call | tf_op jit(solution)/shard_map/solve/pallas_call | solution.py:269
  542.1 0.0 copy-start
  542.1 1.6 copy-done
  543.6 92.6 %gather.1 = (f32[1024,1024]{1,0:T(8,128)S(1)}, f32[1024,1024]{1,0:T(8,128)S(1)}) custom-call(f32[512,1024]{1,0:T(8,128)S(1)} %copy-done), custom_call_target="tpu_custom_call" | custom-call | tf_op jit(solution)/shard_map/gather/pallas_call | solution.py:340
  636.3 0.0 copy-start.1
  636.3 2.0 copy-done.1
  638.2 0.0 copy-start.2
  638.2 1.9 copy-done.2
  640.2 18.0 %finish.1 = f32[1024,1024]{1,0:T(8,128)} custom-call(s32[2]{0:T(128)} %pad_add_fusion.place, f32[1024,1024]{1,0:T(8,128)} %get-tuple-element.20.block, f32[1024,1024]{1,0:T(8,128)} %copy-done.1, f32[1024,1024]{1,0:T(8,128)} %copy-done.2, f32[1024,1024]{1,0:T(8,128)} %get-tuple-element.29.corner), custom_call_target="tpu_custom_call" | custom-call | tf_op jit(solution)/shard_map/finish/pallas_call | solution.py:400
  (3 shorter events, 0.0 us)
Async XLA Ops:
  37.8 7.3 %copy-start.3 = (s32[1,8]{1,0:T(1,128)S(1)}, s32[1,8]{1,0:T(1,128)}, u32[]{:S(2)}) copy-start(s32[1,8]{1,0:T(1,128)} %param.6) | copy-start | bytes 100
  37.8 147.5 %all-to-all-start = ((f32[16,256,256]{2,1,0:T(8,128)}), f32[16,256,256]{2,1,0:T(8,128)}, u32[]{:S(2)}, u32[]{:S(2)}) async-start(f32[16,256,256]{2,1,0:T(8,128)} %get-tuple-element.17), calls=%async_computation | async-start | bytes 8388608 | tf_op jit(solution)/shard_map/all_to_all | solution.py:446
  196.1 46.0 %all-to-all-start.1 = ((f32[2,8,256,256]{3,2,1,0:T(8,128)}), f32[2,8,256,256]{3,2,1,0:T(8,128)}, u32[]{:S(2)}, u32[]{:S(2)}) async-start(f32[2,8,256,256]{3,2,1,0:T(8,128)} %bitcast.29), calls=%async_computation.1 | async-start | bytes 8388608 | tf_op jit(solution)/shard_map/all_to_all | solution.py:448
  201.7 174.3 %all-reduce.2.cloned.1.call-start = ((), (), s32[]{:S(2)}) async-start(), calls=%async_computation.4 | async-start | bytes 8388608 | tf_op jit(solution)/shard_map/psum | solution.py:412
  429.8 95.7 %all-to-all-start.2 = ((f32[4,256,1024]{2,1,0:T(8,128)}), f32[4,256,1024]{2,1,0:T(8,128)}, u32[]{:S(2)}, u32[]{:S(2)}) async-start(f32[4,256,1024]{2,1,0:T(8,128)} %bitcast.28), calls=%async_computation.2 | async-start | bytes 8388608 | tf_op jit(solution)/shard_map/all_to_all | solution.py:466
  542.1 1.6 copy-start
  636.3 2.0 copy-start.1
  638.2 1.9 copy-start.2
Sparse Core Ops, SparseCore 0:
  253.3 122.6 all-reduce.1
